TPU v7x, 32 devices: a whole 2x2x4 slice. The times are simulated.
32 devices in a mesh: view: 8 (over z, y), feat: 4 (over x, core).
Axes of the slice: x: 2, y: 2, z: 4, core: 2. Of those that a mesh axis runs over, the one named last changes fastest.
Arguments:
- points: bfloat16 [512, 768, 128], P('view', 'feat'), may hold values from -6 to 6
- head_weight: bfloat16 [768, 768], P('feat'), may hold values from -0.21875 to 0.21875
- teacher: bfloat16 [768, 16, 1369], P('feat', 'view'), may hold values from -6 to 6
- splat_weight: bfloat16 [16, 64, 74, 128], P('view'), may hold values from 0 to 0.19921875
- block_owner: int32 [16, 16, 4], P('view'), may hold values from 0 to 7, all different within a row; in each aligned block of 32 rows (0 to 31, 32 to 63, ..., all dimensions but the last counted through in order) at most 24 rows name the same one
- block_local: int32 [16, 64], P('view'), may hold values from 0 to 63
- block_row: int32 [16, 64], P('view'), may hold values from 0 to 35, as said below
Outputs:
- grad_points: bfloat16 [512, 768, 128], P('view', 'feat')
- head_grad: float32 [768, 768], P('feat')
Inputs may be any that keep to these rules, and one draw needn't show every extreme that they name: `block_owner`: over the 128 list entries of the views of one index of view, no owner appears more than 24 times, and some owner appears exactly 24 times. `block_row`: each view's list holds every value from 0 to 35 at least once.
All inputs are finite; a program needn't handle non-finite values.
Results may differ from a plain program's by a relative error of at most 0.0064.
Values may be sent and summed in bfloat16 or wider, within the bound.
No kernel may reach another device: no remote copies, remote signals or barrier semaphores. Data moves between devices by JAX's collectives and lax.ppermute only.
A program may use at most 128 MiB of HBM per device.

v0:
```python
import jax
import jax.numpy as jnp
from jax import lax
from jax.sharding import PartitionSpec as P

GRID = 37
BAND = 2
BLOCK = 128


def slot_plan(owners, peer_count, capacity):
    total_requests = owners.shape[0]
    positions = jnp.arange(total_requests, dtype=jnp.int32)
    earlier = (owners[:, None] == owners[None, :]) & (positions[None, :] < positions[:, None])
    slot_rank = jnp.sum(earlier.astype(jnp.int32), axis=1)
    target = owners * capacity + slot_rank
    slot_ids = jnp.arange(peer_count * capacity, dtype=jnp.int32)
    matches = target[None, :] == slot_ids[:, None]
    source = jnp.sum(jnp.where(matches, positions[None, :], 0), axis=1)
    filled = jnp.any(matches, axis=1)
    return (target, source, filled)


def per_device(points, head_weight, teacher, splat_weight, block_owner, block_local, block_row):
    peer_count = lax.axis_size("view")
    local_width = points.shape[1]
    view_count = splat_weight.shape[0]
    visible = splat_weight.shape[1]
    requests = view_count * visible
    capacity = max(3, (3 * requests + 2 * peer_count - 1) // (2 * peer_count))
    owners = block_owner.reshape(requests)
    local_ids = block_local.reshape(requests)
    target, source, filled = slot_plan(owners, peer_count, capacity)
    wanted = jnp.where(filled, jnp.take(local_ids, source), 0)
    columns = jnp.arange(GRID, dtype=jnp.int32)
    row_masks = [
        (block_row[:, :, None] + offset == columns[None, None, :]).astype(jnp.bfloat16)
        for offset in range(BAND)
    ]
    empty_bf = jnp.zeros((), jnp.bfloat16)
    asked_ids = lax.all_to_all(wanted, "view", split_axis=0, concat_axis=0, tiled=True)
    sent_rows = jnp.take(points, asked_ids, axis=0)
    arrived = lax.all_to_all(sent_rows, "view", split_axis=0, concat_axis=0, tiled=True)
    fetched = jnp.take(arrived, target, axis=0).reshape(view_count, visible, local_width, BLOCK)
    contrib = jnp.einsum(
        "vjcp,vjdp->vjcd", splat_weight, fetched, preferred_element_type=jnp.float32
    ).astype(jnp.bfloat16)
    rendered = jnp.zeros((view_count, GRID, GRID, local_width), jnp.float32)
    for offset in range(BAND):
        band_part = contrib[:, :, offset * GRID : (offset + 1) * GRID, :]
        rendered = rendered + jnp.einsum(
            "vjr,vjcd->vrcd", row_masks[offset], band_part, preferred_element_type=jnp.float32
        )
    rendered_rows = rendered.astype(jnp.bfloat16).reshape(view_count * GRID * GRID, local_width)
    pixel_rows = rendered_rows.shape[0]
    teacher_width = head_weight.shape[1]
    local_teacher = teacher.shape[0]
    contract_first = (((0,), (1,)), ((), ()))
    head_full = lax.all_gather(head_weight, "feat", axis=0, tiled=True)
    head_cols = lax.dynamic_slice_in_dim(
        head_full, lax.axis_index("feat") * local_teacher, local_teacher, 1
    )
    head_part = head_cols
    projected = lax.dot_general(
        head_part,
        lax.all_gather(rendered_rows, "feat", axis=1, tiled=True),
        contract_first,
        preferred_element_type=jnp.float32,
    )
    square_sum = lax.psum(jnp.sum(projected * projected, axis=0), "feat")
    scale_rows = jnp.sqrt(square_sum / teacher_width + 1e-06)
    normed = projected / scale_rows[None, :]
    target_feat = teacher.reshape(local_teacher, pixel_rows).astype(jnp.float32)
    residual = normed - target_feat
    row_dot = lax.psum(jnp.sum(residual * normed, axis=0), "feat")
    grad_proj = (
        (residual - normed * (row_dot / teacher_width)[None, :]) / scale_rows[None, :]
    ).astype(jnp.bfloat16)
    shard_part = lax.all_gather(grad_proj, "feat", axis=0, tiled=True)
    head_part = head_weight
    grad_image = lax.dot_general(
        shard_part, head_part, contract_first, preferred_element_type=jnp.float32
    )
    column_part = lax.dot_general(
        rendered_rows, shard_part, contract_first, preferred_element_type=jnp.float32
    )
    grad_head = column_part
    grad_image, grad_head = (grad_image, grad_head)
    head_grad = lax.psum(grad_head, "view") / (view_count * peer_count * GRID)
    grad_image = grad_image.astype(jnp.bfloat16).reshape(view_count, GRID, GRID, local_width)
    pieces = [
        jnp.einsum("vjr,vrcd->vjcd", row_mask, grad_image, preferred_element_type=jnp.float32)
        for row_mask in row_masks
    ]
    grad_contrib = jnp.concatenate(pieces, axis=2).astype(jnp.bfloat16)
    grad_block = jnp.einsum(
        "vjcp,vjcd->vjdp", splat_weight, grad_contrib, preferred_element_type=jnp.float32
    ).astype(jnp.bfloat16)
    grad_block = grad_block.reshape(requests, local_width, BLOCK)
    packed = jnp.where(filled[:, None, None], jnp.take(grad_block, source, axis=0), empty_bf)
    landed = lax.all_to_all(packed, "view", split_axis=0, concat_axis=0, tiled=True)
    summed = jax.ops.segment_sum(
        landed.astype(jnp.float32), asked_ids, num_segments=points.shape[0]
    )
    grad_points = summed.astype(jnp.bfloat16)
    return (grad_points, head_grad)


def solution(mesh):
    placed = (
        P("view", "feat", None),
        P("feat", None),
        P("feat", "view", None),
        P("view", None, None, None),
        P("view", None, None),
        P("view", None),
        P("view", None),
    )
    return jax.shard_map(
        per_device,
        mesh=mesh,
        in_specs=placed,
        out_specs=(P("view", "feat", None), P("feat", None)),
        check_vma=False,
    )
```

profile of v0, /device:TPU:0, one launch (start us, length us, event | category | flops | bytes accessed | tf_op | source)
XLA Modules:
  0.0 750.6 jit_solution(4168131016582856844)
XLA Ops:
  7.2 0.9 copy.39
  8.2 0.2 convert_reduce_fusion
  8.6 0.8 reshape.193
  9.6 1.6 gather_fusion
  11.2 13.5 %all_to_all.19 = s32[8,24,1]{1,2,0:T(1,128)S(1)} all-to-all(s32[8,24,1]{1,2,0:T(1,128)S(1)} %bitcast.36), channel_id=1, replica_groups=mesh['view'=8,'feat'=4] {'view'}, dimensions={0} | all-to-all | bytes 1536 | tf_op jit(solution)/shard_map/all_to_all | solution.py:41
  24.9 0.5 broadcast.172
  25.4 0.7 reduce.5
  26.2 9.6 %gather_fusion.1 = bf16[192,192,128]{2,1,0:T(8,128)(2,1)} fusion(bf16[64,192,128]{2,1,0:T(8,128)(2,1)S(1)} %copy-done, s32[1024]{0:T(1024)S(1)} %pad_clamp_fusion.1), kind=kCustom, calls=%fused_computation.1 | custom fusion | bytes 18875136 | tf_op jit(solution)/shard_map/jit(_take)/gather | solution.py:42
  35.7 8.2 %broadcast_select_fusion = bf16[192,192,128]{2,1,0:T(8,128)(2,1)} fusion(bf16[192,192,128]{2,1,0:T(8,128)(2,1)} %gather_fusion.1, pred[192]{0:T(512)(128)(4,1)S(1)} %compare_and_fusion), kind=kLoop, calls=%fused_computation.6 | loop fusion | flops 4718592 | bytes 18874560 | tf_op jit(solution)/shard_map/jit(_take)/select_n | solution.py:42
  44.0 5.2 all-to-all-start.1
  49.2 0.7 all-gather.4.cloned.1.call-update
  49.9 0.2 all-gather.6.cloned.1.call-start
  50.6 203.0 %all-to-all-done.1 = bf16[192,192,128]{2,1,0:T(8,128)(2,1)} async-done(((bf16[192,192,128]{2,1,0:T(8,128)(2,1)}), bf16[192,192,128]{2,1,0:T(8,128)(2,1)}, u32[]{:S(2)}, u32[]{:S(2)}) %all-to-all-start.1) | async-done | bytes 9437216 | tf_op jit(solution)/shard_map/all_to_all | solution.py:43
  253.5 7.7 %gather_fusion.2 = bf16[128,192,128]{2,1,0:T(8,128)(2,1)} fusion(bf16[192,192,128]{2,1,0:T(8,128)(2,1)} %all-to-all-done.1, s32[1024]{0:T(1024)S(1)} %pad_clamp_fusion), kind=kCustom, calls=%fused_computation.2 | custom fusion | bytes 12583424 | tf_op jit(solution)/shard_map/jit(_take)/gather | solution.py:44
  261.3 9.3 %convert_bitcast_fusion = bf16[2,64,74,192]{3,2,1,0:T(8,128)(2,1)} fusion(bf16[2,64,192,128]{3,2,1,0:T(8,128)(2,1)} %bitcast.34, pred[2,64]{1,0:T(4,128)(4,1)S(1)} %compare_and_fusion.1, bf16[2,64,74,128]{3,1,2,0:T(8,128)(2,1)S(1)} %copy-done.4), kind=kOutput, calls=%fused_computation.12 | convolution fusion | flops 470532096 | bytes 12353664 | tf_op jit(solution)/shard_map/vjcp,vjdp->vjcd/dot_general | solution.py:45
  270.6 4.3 fusion.39
  274.9 0.6 fusion.11
  275.4 0.7 add_convert_fusion
  276.1 0.3 copy.46
  276.4 0.7 reshape.194
  277.2 1.9 copy.47
  279.2 1.7 reshape.197
  280.9 32.7 %all-gather.6.cloned.1.call-done = bf16[2738,768]{0,1:T(8,128)(2,1)} async-done(((bf16[2738,192]{0,1:T(8,128)(2,1)}), bf16[2738,768]{0,1:T(8,128)(2,1)}) %all-gather.6.cloned.1.call-update) | async-done | bytes 4205584 | tf_op jit(solution)/shard_map/all_gather | solution.py:66
  313.6 3.6 multiply_reduce_fusion.1
  317.1 10.2 %psum.21 = f32[2738]{0:T(1024)S(1)} all-reduce(f32[2738]{0:T(1024)S(1)} %get-tuple-element.4), channel_id=1, replica_groups=mesh['view'=8,'feat'=4] {'feat'}, use_global_device_ids=true, to_apply=%region_4.5 | all-reduce | flops 2738 | bytes 21904 | tf_op jit(solution)/shard_map/psum | solution.py:70
  327.3 1.9 multiply_reduce_fusion
  329.2 10.3 %psum.22 = f32[2738]{0:T(1024)S(1)} all-reduce(f32[2738]{0:T(1024)S(1)} %multiply_reduce_fusion), channel_id=1, replica_groups=mesh['view'=8,'feat'=4] {'feat'}, use_global_device_ids=true, to_apply=%region_6.7 | all-reduce | flops 2738 | bytes 21904 | tf_op jit(solution)/shard_map/psum | solution.py:75
  339.6 3.1 divide_convert_fusion
  342.7 36.4 %all-gather.8.cloned.1.call-done = bf16[768,2738]{1,0:T(8,128)(2,1)} async-done(((bf16[192,2738]{1,0:T(8,128)(2,1)}), bf16[768,2738]{1,0:T(8,128)(2,1)}) %all-gather.8.cloned.1.call-update) | async-done | bytes 4205584 | tf_op jit(solution)/shard_map/all_gather | solution.py:79
  379.1 3.2 convolution_convert_fusion
  382.4 1.2 copy.48
  383.6 0.7 reshape.195
  384.3 0.8 convolution_convert_fusion.1
  385.1 0.8 convolution_convert_fusion.2
  386.0 0.8 pad_maximum_fusion
  386.8 0.9 copy-done.5
  387.7 7.4 fusion.5
  395.1 12.4 %gather_fusion.3 = bf16[192,192,128]{2,1,0:T(8,128)(2,1)} fusion(bf16[128,192,128]{2,1,0:T(8,128)(2,1)} %bitcast.33, s32[1024]{0:T(1024)S(1)} %pad_clamp_fusion.2), kind=kCustom, calls=%fused_computation.3 | custom fusion | bytes 18875136 | tf_op jit(solution)/shard_map/jit(_take)/gather | solution.py:100
  407.5 9.9 %select_select_fusion = bf16[192,192,128]{2,1,0:T(8,128)(2,1)} fusion(bf16[192,192,128]{2,1,0:T(8,128)(2,1)} %gather_fusion.3, pred[192]{0:T(512)(128)(4,1)S(1)} %compare_and_fusion.2, pred[192]{0:T(512)(128)(4,1)S(1)} %fusion.23), kind=kLoop, calls=%fused_computation.5 | loop fusion | flops 9437184 | bytes 18874752 | tf_op jit(solution)/shard_map/jit(_where)/select_n | solution.py:100
  417.4 5.6 all-to-all-start.2
  423.1 0.3 all-reduce.2.cloned.1.call-start
  423.4 4.6 fusion.40
  428.0 246.2 %all-reduce.2.cloned.1.call-done = f32[192,768]{1,0:T(8,128)} async-done(((f32[192,768]{1,0:T(8,128)}), f32[192,768]{1,0:T(8,128)}) %all-reduce.2.cloned.1.call-update) | async-done | bytes 589840 | tf_op jit(solution)/shard_map/psum | solution.py:89
  674.3 1.9 broadcast_multiply_fusion
  676.2 12.4 %convert_element_type.45 = f32[192,192,128]{2,1,0:T(8,128)} convert(bf16[192,192,128]{2,1,0:T(8,128)(2,1)} %all-to-all-done.2) | non-fusion elementwise | flops 4718592 | bytes 28311552 | tf_op jit(solution)/shard_map/convert_element_type | solution.py:103
  688.6 3.4 broadcast_in_dim.79
  692.0 47.0 %scatter_fusion = f32[64,192,128]{2,1,0:T(8,128)} fusion(f32[64,192,128]{2,1,0:T(8,128)} %broadcast_in_dim.79, s32[192]{0:T(256)S(1)} %reshape.232, f32[192,192,128]{2,1,0:T(8,128)} %convert_element_type.45), kind=kCustom, calls=%fused_computation.4 | custom fusion | flops 4718592 | bytes 56623872 | tf_op jit(solution)/shard_map/scatter-add | solution.py:102
  739.0 5.0 convert_element_type.46
  (53 shorter events, 1.4 us)
Async XLA Ops:
  7.2 19.0 %copy-start = (bf16[64,192,128]{2,1,0:T(8,128)(2,1)S(1)}, bf16[64,192,128]{2,1,0:T(8,128)(2,1)}, u32[]{:S(2)}) copy-start(bf16[64,192,128]{2,1,0:T(8,128)(2,1)} %param.7) | copy-start | bytes 9437188
  44.0 6.1 copy-start.8
  44.0 6.5 copy-start.9
  44.0 209.6 %all-to-all-start.1 = ((bf16[192,192,128]{2,1,0:T(8,128)(2,1)}), bf16[192,192,128]{2,1,0:T(8,128)(2,1)}, u32[]{:S(2)}, u32[]{:S(2)}) async-start(bf16[192,192,128]{2,1,0:T(8,128)(2,1)} %broadcast_select_fusion), calls=%async_computation.1 | async-start | bytes 18874368 | tf_op jit(solution)/shard_map/all_to_all | solution.py:43
  49.2 231.7 %all-gather.4.cloned.1.call-start = ((), (), s32[]{:S(2)}) async-start(), calls=%async_computation.3 | async-start | bytes 1474560 | tf_op jit(solution)/shard_map/all_gather | solution.py:59
  49.9 263.7 %all-gather.6.cloned.1.call-start = ((), (), s32[]{:S(2)}) async-start(), calls=%async_computation.4 | async-start | bytes 5406720 | tf_op jit(solution)/shard_map/all_gather | solution.py:66
  50.6 210.7 %copy-start.4 = (bf16[2,64,74,128]{3,1,2,0:T(8,128)(2,1)S(1)}, bf16[2,64,74,128]{3,1,2,0:T(8,128)(2,1)}, u32[]{:S(2)}) copy-start(bf16[2,64,74,128]{3,1,2,0:T(8,128)(2,1)} %param.10) | copy-start | bytes 7274500
  277.2 3.7 copy-start.2
  277.2 2.0 copy-start.6
  279.1 100.0 %all-gather.8.cloned.1.call-start = ((), (), s32[]{:S(2)}) async-start(), calls=%async_computation.5 | async-start | bytes 5406720 | tf_op jit(solution)/shard_map/all_gather | solution.py:79
  339.6 39.5 %copy-start.7 = (bf16[192,768]{1,0:T(8,128)(2,1)S(1)}, bf16[192,768]{1,0:T(8,128)(2,1)}, u32[]{:S(2)}) copy-start(bf16[192,768]{1,0:T(8,128)(2,1)} %param.8) | copy-start | bytes 884740
  386.0 1.7 copy-start.5
  417.4 6.0 copy-start.3
  417.4 258.8 %all-to-all-start.2 = ((bf16[192,192,128]{2,1,0:T(8,128)(2,1)}), bf16[192,192,128]{2,1,0:T(8,128)(2,1)}, u32[]{:S(2)}, u32[]{:S(2)}) async-start(bf16[192,192,128]{2,1,0:T(8,128)(2,1)} %select_select_fusion), calls=%async_computation.2 | async-start | bytes 18874368 | tf_op jit(solution)/shard_map/all_to_all | solution.py:101
  423.1 251.2 %all-reduce.2.cloned.1.call-start = ((), (), s32[]{:S(2)}) async-start(), calls=%async_computation.6 | async-start | bytes 1179648 | tf_op jit(solution)/shard_map/psum | solution.py:89
  692.0 52.1 %copy-start.1 = (bf16[64,192,128]{2,1,0:T(8,128)(2,1)S(1)}, bf16[64,192,128]{2,1,0:T(8,128)(2,1)}, u32[]{:S(2)}) copy-start(bf16[64,192,128]{2,1,0:T(8,128)(2,1)} %param.7) | copy-start | bytes 9437188
Sparse Core Ops, SparseCore 0:
  51.6 18.7 all-gather.3
  279.3 34.2 all-gather.5
  342.8 36.2 all-gather.7
  428.2 246.0 all-reduce.1
where the time goes:
time: 753 us; the launch traced here: 751 us
  waiting for transfers between devices  519 us (69%)
  other arithmetic  91.5 us (12%)
  local copies, waits for them, and re-layouts  49.5 us (7%)
  blocking collectives  34.1 us (5%)
  matrix products  31.1 us (4%)
  between operations  14 us (2%)
  starting transfers between devices  11.4 us (2%)
    psum x1, waiting for transfers between devices, per_device(): head_grad = lax.psum(grad_head, 'view') / (view_count * peer_count * GRID)  246 us
    all_to_all x1, waiting for transfers between devices, per_device(): lax.all_to_all(sent_rows, 'view', split_axis=0, concat_axis=0, tiled=True)  203 us
    scatter-add x1, other arithmetic, per_device(): jax.ops.segment_sum(landed.astype(jnp.float32), asked_ids, num_segments=p...  47 us
    all_gather x1, waiting for transfers between devices, per_device(): shard_part = lax.all_gather(grad_proj, 'feat', axis=0, tiled=True)  36.4 us
    all_gather x1, waiting for transfers between devices, per_device(): lax.all_gather(rendered_rows, 'feat', axis=1, tiled=True)  32.7 us
  transfers between devices with their start and end apart: 6, of which 4 were waited for; matrix products, arithmetic and copies ran while one was open for 5% of the time, Pallas kernels for 0%

commit v1 on v0

--- a/solution.py
+++ b/solution.py
@@ -1,11 +1,15 @@
 import jax
 import jax.numpy as jnp
 from jax import lax
+from jax.experimental import pallas as pl
+from jax.experimental.pallas import tpu as pltpu
 from jax.sharding import PartitionSpec as P
 
 GRID = 37
 BAND = 2
 BLOCK = 128
+GROUP = 4
+VMEM_BYTES = 48 * 1024 * 1024
 
 
 def slot_plan(owners, peer_count, capacity):
@@ -21,7 +25,7 @@
     return (target, source, filled)
 
 
-def per_device(points, head_weight, teacher, splat_weight, block_owner, block_local, block_row):
+def per_device_listed(points, head_weight, teacher, splat_weight, block_owner, block_local, block_row):
     peer_count = lax.axis_size("view")
     local_width = points.shape[1]
     view_count = splat_weight.shape[0]
@@ -106,7 +110,375 @@
     return (grad_points, head_grad)
 
 
+def shifted(weight, start):
+    rows = jnp.concatenate([weight.astype(jnp.float32), jnp.zeros((8, BLOCK), jnp.float32)], axis=0)
+    return pltpu.roll(rows, lax.rem(start, 8), 0).astype(jnp.bfloat16)
+
+
+def rows_at(start, band_rows):
+    return pl.ds(pl.multiple_of((start // 8) * 8, 8), band_rows + 8)
+
+
+def render_kernel(
+    half_rows, band_rows, count_ref, block_ref, place_ref, where_ref, weight_ref, points_ref, *rest
+):
+    outs, acc = rest[:-1], rest[-1]
+    width = points_ref.shape[1]
+    acc[...] = jnp.zeros_like(acc)
+
+    def group(step, carry):
+        parts = []
+        for t in range(GROUP):
+            slot = step * GROUP + t
+            parts.append(
+                lax.dot_general(
+                    shifted(weight_ref[where_ref[slot]], place_ref[slot]),
+                    points_ref[block_ref[slot]],
+                    (((1,), (1,)), ((), ())),
+                    preferred_element_type=jnp.float32,
+                )
+            )
+        for t in range(GROUP):
+            rows = rows_at(place_ref[step * GROUP + t], band_rows)
+            acc[rows, 0:width] += parts[t]
+        return carry
+
+    lax.fori_loop(0, (count_ref[0] + GROUP - 1) // GROUP, group, 0)
+    lane = lax.broadcasted_iota(jnp.int32, (half_rows, 128), 1)
+    for u, out in enumerate(outs):
+        first = acc[2 * u * half_rows : (2 * u + 1) * half_rows, :]
+        second = pltpu.roll(acc[(2 * u + 1) * half_rows : (2 * u + 2) * half_rows, :], 64, 1)
+        out[:, 0:128] = first[:, 0:128].astype(out.dtype)
+        out[:, 128:256] = jnp.where(lane < 64, first[:, 128:256], second[:, 0:128]).astype(out.dtype)
+        out[:, 256:384] = second[:, 128:256].astype(out.dtype)
+
+
+def render(count, block, place, where, weight, points, view_count, half_rows):
+    width = points.shape[1]
+    band_rows = weight.shape[1]
+    smem = pl.BlockSpec(memory_space=pltpu.SMEM)
+    vmem = pl.BlockSpec(memory_space=pltpu.VMEM)
+    image = jax.ShapeDtypeStruct((half_rows, 2 * width), jnp.bfloat16)
+    return pl.pallas_call(
+        lambda *refs: render_kernel(half_rows, band_rows, *refs),
+        out_shape=[image] * view_count,
+        in_specs=[smem] * 4 + [vmem] * 2,
+        out_specs=[vmem] * view_count,
+        scratch_shapes=[pltpu.VMEM((2 * view_count * half_rows + band_rows + 8, 256), jnp.float32)],
+        compiler_params=pltpu.CompilerParams(vmem_limit_bytes=VMEM_BYTES),
+        name="render_blocks",
+    )(count, block, place, where, weight, points)
+
+
+def loss_kernel(teacher_width, parts_ref, head_ref, teacher_ref, image_ref, grad_ref):
+    rows, packed = parts_ref.shape[1], parts_ref.shape[2]
+    width = packed // 2
+    lane = lax.broadcasted_iota(jnp.int32, (rows, packed), 1)
+    head = head_ref[...]
+    halves = [[], []]
+    for pair in range(2):
+        one = parts_ref[2 * pair].astype(jnp.float32)
+        two = parts_ref[2 * pair + 1].astype(jnp.float32)
+        halves[0].append(jnp.where(lane < width, one, pltpu.roll(two, width, 1)))
+        halves[1].append(jnp.where(lane < width, pltpu.roll(one, width, 1), two))
+    rendered_all, grad_all, images = [], [], []
+    for half in range(2):
+        rendered = jnp.concatenate(halves[half], axis=1).astype(jnp.bfloat16)
+        projected = jnp.dot(rendered, head, preferred_element_type=jnp.float32)
+        square = jnp.sum(projected * projected, axis=1, keepdims=True)
+        scale = jnp.sqrt(square / teacher_width + 1e-06)
+        normed = projected / scale
+        residual = normed - teacher_ref[half].astype(jnp.float32)
+        inner = jnp.sum(residual * normed, axis=1, keepdims=True) / teacher_width
+        grad_proj = ((residual - normed * inner) / scale).astype(jnp.bfloat16)
+        images.append(
+            lax.dot_general(
+                grad_proj, head, (((1,), (1,)), ((), ())), preferred_element_type=jnp.float32
+            )
+        )
+        rendered_all.append(rendered)
+        grad_all.append(grad_proj)
+    for pair in range(2):
+        cols = slice(2 * pair * width, 2 * (pair + 1) * width)
+        first, second = images[0][:, cols], images[1][:, cols]
+        image_ref[2 * pair] = jnp.where(lane < width, first, pltpu.roll(second, width, 1)).astype(
+            image_ref.dtype
+        )
+        image_ref[2 * pair + 1] = jnp.where(
+            lane < width, pltpu.roll(first, width, 1), second
+        ).astype(image_ref.dtype)
+    grad_ref[...] = lax.dot_general(
+        jnp.concatenate(rendered_all, axis=0),
+        jnp.concatenate(grad_all, axis=0),
+        (((0,), (0,)), ((), ())),
+        preferred_element_type=jnp.float32,
+    )
+
+
+def loss(parts, head, teacher):
+    vmem = pl.BlockSpec(memory_space=pltpu.VMEM)
+    teacher_width = head.shape[1]
+    return pl.pallas_call(
+        lambda *refs: loss_kernel(teacher_width, *refs),
+        out_shape=[
+            jax.ShapeDtypeStruct(parts.shape, jnp.bfloat16),
+            jax.ShapeDtypeStruct(head.shape, jnp.float32),
+        ],
+        in_specs=[vmem] * 3,
+        out_specs=[vmem] * 2,
+        compiler_params=pltpu.CompilerParams(vmem_limit_bytes=VMEM_BYTES),
+        name="loss_rows",
+    )(parts, head, teacher)
+
+
+def pull_kernel(
+    half_rows, band_rows, view_count, first, last,
+    count_ref, block_ref, place_ref, where_ref, weight_ref, image_refs, old_ref, out_ref, image, acc
+):
+    step_of = pl.program_id(0)
+    width = acc.shape[1]
+    blocks = out_ref.shape[0]
+
+    @pl.when(step_of == 0)
+    def _():
+        if first:
+            acc[...] = jnp.zeros_like(acc)
+        else:
+            acc[0:blocks] = old_ref[...]
+
+    for u in range(view_count):
+        packed = image_refs[u][0].astype(jnp.float32)
+        image[2 * u * half_rows : (2 * u + 1) * half_rows, :] = packed[:, 0:256]
+        tail = jnp.concatenate([packed[:, 128:384]], axis=1)
+        image[(2 * u + 1) * half_rows : (2 * u + 2) * half_rows, :] = pltpu.roll(tail, 192, 1)
+
+    slots = weight_ref.shape[1]
+    base = step_of * slots
+
+    def group(step, carry):
+        parts = []
+        for t in range(GROUP):
+            slot = base + step * GROUP + t
+            rows = rows_at(place_ref[slot], band_rows)
+            parts.append(
+                lax.dot_general(
+                    image[rows, 0:width].astype(jnp.bfloat16),
+                    shifted(weight_ref[0, where_ref[slot]], place_ref[slot]),
+                    (((0,), (0,)), ((), ())),
+                    preferred_element_type=jnp.float32,
+                )
+            )
+        for t in range(GROUP):
+            slot = base + step * GROUP + t
+            acc[block_ref[slot]] += parts[t]
+        return carry
+
+    lax.fori_loop(0, (count_ref[step_of] + GROUP - 1) // GROUP, group, 0)
+
+    @pl.when(step_of == pl.num_programs(0) - 1)
+    def _():
+        out_ref[...] = acc[0:blocks].astype(out_ref.dtype)
+
+
+def pull(count, block, place, where, weight, images, old, blocks, width, last):
+    view_count = len(images)
+    peers, slots, band_rows, points = weight.shape
+    half_rows = images[0].shape[1]
+    first = old is None
+    smem = pl.BlockSpec(memory_space=pltpu.SMEM)
+    vmem = pl.BlockSpec(memory_space=pltpu.VMEM)
+
+    def body(count_ref, block_ref, place_ref, where_ref, weight_ref, *rest):
+        image_refs, rest = rest[:view_count], rest[view_count:]
+        if first:
+            rest = (None,) + rest
+        pull_kernel(
+            half_rows, band_rows, view_count, first, last,
+            count_ref, block_ref, place_ref, where_ref, weight_ref, image_refs, *rest
+        )
+
+    args = [count, block, place, where, weight] + list(images)
+    in_specs = [smem] * 4 + [pl.BlockSpec((1, slots, band_rows, points), lambda i: (i, 0, 0, 0))]
+    in_specs += [pl.BlockSpec((1,) + images[0].shape[1:], lambda i: (i, 0, 0))] * view_count
+    if not first:
+        args.append(old)
+        in_specs.append(vmem)
+    return pl.pallas_call(
+        body,
+        grid=(peers,),
+        out_shape=jax.ShapeDtypeStruct((blocks, width, points), jnp.bfloat16 if last else jnp.float32),
+        in_specs=in_specs,
+        out_specs=vmem,
+        scratch_shapes=[
+            pltpu.VMEM((2 * view_count * half_rows + band_rows + 8, 256), jnp.float32),
+            pltpu.VMEM((blocks + 1, width, points), jnp.float32),
+        ],
+        compiler_params=pltpu.CompilerParams(vmem_limit_bytes=VMEM_BYTES),
+        name="pull_blocks",
+    )(*args)
+
+
+def total(*terms):
+    acc = terms[0].astype(jnp.float32)
+    for term in terms[1:]:
+        acc = acc + term.astype(jnp.float32)
+    return acc.astype(jnp.bfloat16)
+
+
+def in_order(own_first, other):
+    index, mine = own_first
+    return jnp.where(
+        index == 0, jnp.concatenate([mine, other], 0), jnp.concatenate([other, mine], 0)
+    )
+
+
+def per_device(points, head_weight, teacher, splat_weight, block_owner, block_local, block_row):
+    peers, sides = lax.axis_size("view"), lax.axis_size("feat")
+    blocks, width = points.shape[0], points.shape[1]
+    view_count, visible, band_rows = splat_weight.shape[:3]
+    requests = view_count * visible
+    capacity = max(3, (3 * requests + 2 * peers - 1) // (2 * peers))
+    quarter = -(-capacity // sides)
+    slots = quarter * sides
+    pixels = teacher.shape[2]
+    unit = 2 * sides * 16
+    padded = -(-pixels // unit) * unit
+    half_rows = padded // 2
+    me, side = lax.axis_index("view"), lax.axis_index("feat")
+    line, across, core = me // 2, side // 2, side % 2
+
+    def hop(value, axis, pairs):
+        return lax.ppermute(value, axis, pairs)
+
+    def swap(value, axis, k):
+        size = peers if axis == "view" else sides
+        return hop(value, axis, [(i, i ^ k) for i in range(size)])
+
+    def along(value, moves):
+        return hop(value, "view", [(2 * a + y, 2 * b + y) for a, b in moves for y in range(2)])
+
+    ints = jnp.int32
+    owners = block_owner.reshape(requests)
+    positions = jnp.arange(requests, dtype=ints)
+    earlier = (owners[:, None] == owners[None, :]) & (positions[None, :] < positions[:, None])
+    rank = jnp.sum(earlier.astype(ints), axis=1)
+    peer_ids = me ^ jnp.arange(peers, dtype=ints)
+    send_ranks = side * quarter + jnp.arange(quarter, dtype=ints)
+    match = (owners[None, None, :] == peer_ids[:, None, None]) & (
+        rank[None, None, :] == send_ranks[None, :, None]
+    )
+    source = jnp.sum(jnp.where(match, positions[None, None, :], 0), axis=2)
+    aligned = -(-band_rows // 16) * 16
+    listed = splat_weight.reshape(requests, band_rows, BLOCK)
+    listed = jnp.pad(listed, ((0, 0), (0, aligned - band_rows), (0, 0)))
+    packed = jnp.take(listed, source.reshape(peers * quarter), axis=0).reshape(
+        peers, quarter, aligned, BLOCK
+    )
+
+    view_of = positions // visible
+    start = view_of * padded + block_row.reshape(requests) * GRID
+    told = jnp.stack([owners, rank, block_local.reshape(requests), start])
+    heard = lax.all_gather(told, "view", axis=0)
+    heard = jnp.take(heard, peer_ids, axis=0)
+    slot_ids = jnp.arange(slots, dtype=ints)
+    asked = (heard[:, None, 0, :] == me) & (heard[:, None, 1, :] == slot_ids[None, :, None])
+    filled = jnp.any(asked, axis=2)
+    counts = jnp.sum(filled.astype(ints), axis=1)
+    block_of = jnp.sum(jnp.where(asked, heard[:, None, 2, :], 0), axis=2)
+    place_of = jnp.where(
+        filled, jnp.sum(jnp.where(asked, heard[:, None, 3, :], 0), axis=2), view_count * padded
+    )
+    pull_of = jnp.where(filled, block_of, blocks)
+    turn = (slot_ids // quarter) ^ side
+    turn = (turn % 2) * 2 + turn // 2
+    where_of = turn * quarter + slot_ids % quarter
+
+    weights = {}
+    for j in (3, 2, 1, 0):
+        got = jnp.stack([swap(packed[k], "view", k) if k else packed[k] for k in (2 * j, 2 * j + 1)])
+        got = jnp.concatenate([got, swap(got, "feat", 2)], axis=1)
+        weights[j] = jnp.concatenate([got, swap(got, "feat", 1)], axis=1)
+
+    head = jnp.concatenate([head_weight, swap(head_weight, "feat", 2)], axis=0)
+    head = jnp.concatenate([head, swap(head, "feat", 1)], axis=0)
+    seventh = half_rows // sides
+    target = jnp.pad(teacher, ((0, 0), (0, 0), (0, padded - pixels)))
+    target = target.reshape(width, view_count, 2, sides, seventh).transpose(3, 1, 2, 4, 0)
+    order = side ^ jnp.arange(sides, dtype=ints)
+    target = jnp.take(target, order, axis=0)
+    target = [swap(target[d], "feat", d) if d else target[d] for d in range(sides)]
+    target = jnp.take(jnp.stack(target), order, axis=0)
+    target = target.transpose(1, 2, 3, 0, 4).reshape(view_count, 2, seventh, sides * width)
+
+    kept, sent = {}, {}
+    for j in (3, 2, 1, 0):
+        for k, into in ((2 * j + 1, sent), (2 * j, kept)):
+            into[j] = render(
+                counts[k : k + 1], block_of[k], place_of[k], where_of, weights[j][k - 2 * j], points,
+                view_count, half_rows,
+            )
+    rendered = []
+    for u in range(view_count):
+        pair = {j: (kept[j][u], swap(sent[j][u], "view", 1)) for j in (3, 2, 1, 0)}
+        far = along(total(*pair[3]), [(0, 1), (3, 2)])
+        mid = total(*pair[2], far)
+        inward = along(mid, [(0, 1), (3, 2)])
+        between = along(mid, [(1, 2), (2, 1)])
+        near = along(total(*pair[1], between), [(0, 1), (1, 0), (2, 3), (3, 2)])
+        centre = along(total(*pair[3], inward), [(1, 2), (2, 1)])
+        rendered.append(total(*pair[0], near, centre))
+
+    grads, images = [], []
+    side_rows = half_rows // 2
+    for u in range(view_count):
+        whole = rendered[u]
+        mine = lax.dynamic_slice_in_dim(whole, across * side_rows, side_rows, 0)
+        other = lax.dynamic_slice_in_dim(whole, (1 - across) * side_rows, side_rows, 0)
+        both = jnp.stack([mine, swap(other, "feat", 2)])
+        mine = lax.dynamic_slice_in_dim(both, core * seventh, seventh, 1)
+        other = lax.dynamic_slice_in_dim(both, (1 - core) * seventh, seventh, 1)
+        parts = jnp.concatenate([mine, swap(other, "feat", 1)], axis=0)
+        image, grad = loss(parts, head, target[u])
+        grads.append(grad)
+        back = swap(image[2:4], "feat", 1)
+        rows = [in_order((core, image[i]), back[i]) for i in range(2)]
+        images.append(in_order((across, rows[0]), swap(rows[1], "feat", 2)))
+
+    grad = grads[0]
+    for more in grads[1:]:
+        grad = grad + more
+    grad = grad.reshape(2, 2, width, grad.shape[1])
+    grad = grad[0] + swap(grad[1], "feat", 1)
+    grad = grad[0] + swap(grad[1], "feat", 2)
+    grad = lax.psum(grad, "view")
+    head_grad = grad / (view_count * peers * GRID)
+
+    middle = (line == 1) | (line == 2)
+    chunks = {j: [] for j in range(4)}
+    for u in range(view_count):
+        own = images[u]
+        near = along(own, [(0, 1), (1, 0), (2, 3), (3, 2)])
+        centre = along(own, [(1, 2), (2, 1)])
+        out_near = along(centre, [(1, 0), (2, 3)])
+        cross = along(near, [(1, 2), (2, 1)])
+        out_far = along(cross, [(1, 0), (2, 3)])
+        for j, value in enumerate(
+            (own, near, jnp.where(middle, cross, out_near), jnp.where(middle, centre, out_far))
+        ):
+            chunks[j].append(jnp.stack([value, swap(value, "view", 1)]))
+    acc = None
+    for j in range(4):
+        ks = slice(2 * j, 2 * j + 2)
+        acc = pull(
+            counts[ks], pull_of[ks].reshape(-1), place_of[ks].reshape(-1), jnp.tile(where_of, 2),
+            weights[j], chunks[j], acc, blocks, width, j == 3,
+        )
+    return (acc, head_grad)
+
+
 def solution(mesh):
+    size = mesh.shape
+    paired = size["view"] == 8 and size["feat"] == 4
     placed = (
         P("view", "feat", None),
         P("feat", None),
@@ -117,7 +489,7 @@
         P("view", None),
     )
     return jax.shard_map(
-        per_device,
+        per_device if paired else per_device_listed,
         mesh=mesh,
         in_specs=placed,
         out_specs=(P("view", "feat", None), P("feat", None)),

time: 753 us -> 463 us (0.61)
  waiting for transfers between devices: 519 us -> 168 us
  starting transfers between devices: 11.4 us -> 86.1 us
  Pallas kernels: 0 us -> 70.7 us
  other arithmetic: 91.5 us -> 42.2 us
  matrix products: 31.1 us -> 0 us
  local copies, waits for them, and re-layouts: 49.5 us -> 36.6 us
    all_to_all x2 -> x0, waiting for transfers between devices: 203 us -> none  [the longest x1 203 us: per_device(): lax.all_to_all(sent_rows, 'view', split_axis=0, concat_axis=0, tiled=True)]
    psum x1, waiting for transfers between devices: 246 us -> 61.4 us  [per_device(): grad = lax.psum(grad, 'view')]
    ppermute x0 -> x66, waiting for transfers between devices: none -> 107 us  [hop(): return lax.ppermute(value, axis, pairs)]
    ppermute x0 -> x66, starting transfers between devices: none -> 86 us  [hop(): return lax.ppermute(value, axis, pairs)]
    pallas_call x0 -> x14, Pallas kernels: none -> 70.7 us  [the longest x4 37.2 us: pull(): pl.pallas_call(body, grid=(peers,), out_shape=jax.ShapeDtypeStruct((block...]
    all_gather x3 -> x0, waiting for transfers between devices: 69.1 us -> none  [the longest x1 36.4 us: per_device(): shard_part = lax.all_gather(grad_proj, 'feat', axis=0, tiled=True)]
    scatter-add x1 -> x0, other arithmetic: 47 us -> none  [per_device(): jax.ops.segment_sum(landed.astype(jnp.float32), asked_ids, num_segments=p...]
    all_gather x0 -> x1, blocking collectives: none -> 35 us  [per_device(): heard = lax.all_gather(told, 'view', axis=0)]
  transfers between devices with their start and end apart: 6 -> 67, of which waited for: 4 -> 23; matrix products, arithmetic and copies ran while one was open for 5% -> 14% of each run, Pallas kernels for 0% -> 14%
where the time goes in v1:
time: 463 us; the launch traced here: 455 us
  waiting for transfers between devices  168 us (36%)
  starting transfers between devices  86.1 us (19%)
  Pallas kernels  70.7 us (15%)
  other arithmetic  42.2 us (9%)
  local copies, waits for them, and re-layouts  36.6 us (8%)
  blocking collectives  35 us (8%)
  between operations  15.8 us (3%)
    ppermute x66, waiting for transfers between devices, hop(): return lax.ppermute(value, axis, pairs)  107 us
    ppermute x66, starting transfers between devices, hop(): return lax.ppermute(value, axis, pairs)  86 us
    psum x1, waiting for transfers between devices, per_device(): grad = lax.psum(grad, 'view')  61.4 us
    pallas_call x4, Pallas kernels, pull(): pl.pallas_call(body, grid=(peers,), out_shape=jax.ShapeDtypeStruct((block...  37.2 us
    all_gather x1, blocking collectives, per_device(): heard = lax.all_gather(told, 'view', axis=0)  35 us
    pallas_call x8, Pallas kernels, render(): pl.pallas_call(lambda *refs: render_kernel(half_rows, band_rows, *refs),...  28.1 us
    unnamed x73, local copies, waits for them, and re-layouts  10.6 us
  transfers between devices with their start and end apart: 67, of which 23 were waited for; matrix products, arithmetic and copies ran while one was open for 14% of the time, Pallas kernels for 14%

profile of v1, /device:TPU:0, one launch (start us, length us, event | category | flops | bytes accessed | tf_op | source)
XLA Modules:
  0.0 454.6 jit_solution(6557759629771722867)
XLA Ops:
  8.9 2.2 copy.48
  16.8 5.1 %collective-permute-start = (bf16[6,80,128]{2,1,0:T(8,128)(2,1)}, bf16[6,80,128]{2,1,0:T(8,128)(2,1)}, u32[]{:S(2)}, u32[]{:S(2)}) collective-permute-start(bf16[6,80,128]{2,1,0:T(8,128)(2,1)} %get-tuple-element.62), channel_id=1, source_target_pairs={{0,24},{4,28},{8,16},{12,20},{16,8},{20,12},{24,0},{28,4},{1,25},{... | collective-permute-start | bytes 368648 | tf_op jit(solution)/shard_map/ppermute | solution.py:351
  27.5 35.0 %all-gather.1 = s32[8,4,128]{2,1,0:T(4,128)S(1)} all-gather(s32[1,4,128]{2,1,0:T(4,128)S(1)} %add_bitcast_fusion), channel_id=2, replica_groups=mesh['view'=8,'feat'=4] {'view'}, dimensions={0}, use_global_device_ids=true | all-gather | bytes 18432 | tf_op jit(solution)/shard_map/all_gather | solution.py:381
  64.8 2.9 reshape.561
  84.4 2.8 collective-permute-done.29
  88.7 5.3 %collective-permute-done.30 = bf16[2,2,176,192]{3,2,1,0:T(8,128)(2,1)S(1)} collective-permute-done((bf16[2,2,176,192]{3,2,1,0:T(8,128)(2,1)S(1)}, bf16[2,2,176,192]{3,2,1,0:T(8,128)(2,1)S(1)}, u32[]{:S(2)}, u32[]{:S(2)}) %collective-permute-start.30) | collective-permute-done | bytes 270368 | tf_op jit(solution)/shard_map/ppermute | solution.py:351
  95.0 5.2 %collective-permute-done.2 = bf16[2,6,80,128]{3,2,1,0:T(8,128)(2,1)} collective-permute-done((bf16[2,6,80,128]{3,2,1,0:T(8,128)(2,1)}, bf16[2,6,80,128]{3,2,1,0:T(8,128)(2,1)}, u32[]{:S(2)}, u32[]{:S(2)}) %collective-permute-start.2) | collective-permute-done | bytes 245792 | tf_op jit(solution)/shard_map/ppermute | solution.py:351
  101.7 3.8 collective-permute-done.15
  106.7 4.1 collective-permute-done.10
  114.3 3.4 render_blocks.15
  123.3 3.5 render_blocks.13
  126.8 3.4 render_blocks.14
  133.0 3.7 collective-permute-start.42
  136.7 7.7 %collective-permute-done.18 = bf16[704,384]{1,0:T(8,128)(2,1)S(1)} collective-permute-done((bf16[704,384]{1,0:T(8,128)(2,1)S(1)}, bf16[704,384]{1,0:T(8,128)(2,1)S(1)}, u32[]{:S(2)}, u32[]{:S(2)}) %collective-permute-start.18) | collective-permute-done | bytes 540704 | tf_op jit(solution)/shard_map/ppermute | solution.py:351
  144.6 3.7 collective-permute-start.19
  148.4 3.4 render_blocks.12
  151.8 3.4 render_blocks.11
  161.3 6.3 %collective-permute-done.17 = bf16[704,384]{1,0:T(8,128)(2,1)S(1)} collective-permute-done((bf16[704,384]{1,0:T(8,128)(2,1)S(1)}, bf16[704,384]{1,0:T(8,128)(2,1)S(1)}, u32[]{:S(2)}, u32[]{:S(2)}) %collective-permute-start.17) | collective-permute-done | bytes 540704 | tf_op jit(solution)/shard_map/ppermute | solution.py:351
  167.6 3.7 collective-permute-start.45
  172.9 3.4 render_blocks.10
  177.1 4.1 render_blocks.9
  181.2 2.8 collective-permute-done.45
  185.7 8.1 %collective-permute-done.22 = bf16[704,384]{1,0:T(8,128)(2,1)S(1)} collective-permute-done((bf16[704,384]{1,0:T(8,128)(2,1)S(1)}, bf16[704,384]{1,0:T(8,128)(2,1)S(1)}, u32[]{:S(2)}, u32[]{:S(2)}) %collective-permute-start.22) | collective-permute-done | bytes 540704 | tf_op jit(solution)/shard_map/ppermute | solution.py:351
  198.6 3.7 collective-permute-start.44
  204.8 9.1 %collective-permute-start.21 = (bf16[704,384]{1,0:T(8,128)(2,1)}, bf16[704,384]{1,0:T(8,128)(2,1)}, u32[]{:S(2)}, u32[]{:S(2)}) collective-permute-start(bf16[704,384]{1,0:T(8,128)(2,1)} %add_convert_fusion.6), channel_id=1, source_target_pairs={{0,8},{4,12},{8,0},{12,4},{16,24},{20,28},{24,16},{28,20},{1,9},{5... | collective-permute-start | bytes 1622024 | tf_op jit(solution)/shard_map/ppermute | solution.py:351
  217.8 2.6 squeeze.162.refs_2_
  220.4 2.6 copy.53
  223.0 2.5 squeeze.157.refs_2_
  226.6 3.7 render_blocks.8
  235.9 5.4 %collective-permute-done.47 = bf16[352,384]{1,0:T(8,128)(2,1)S(1)} collective-permute-done((bf16[352,384]{1,0:T(8,128)(2,1)S(1)}, bf16[352,384]{1,0:T(8,128)(2,1)S(1)}, u32[]{:S(2)}, u32[]{:S(2)}) %collective-permute-start.47) | collective-permute-done | bytes 270368 | tf_op jit(solution)/shard_map/ppermute | solution.py:351
  241.6 5.1 %collective-permute-done.24 = bf16[352,384]{1,0:T(8,128)(2,1)S(1)} collective-permute-done((bf16[352,384]{1,0:T(8,128)(2,1)S(1)}, bf16[352,384]{1,0:T(8,128)(2,1)S(1)}, u32[]{:S(2)}, u32[]{:S(2)}) %collective-permute-start.24) | collective-permute-done | bytes 270368 | tf_op jit(solution)/shard_map/ppermute | solution.py:351
  247.8 2.7 loss_rows.3
  251.5 2.7 loss_rows.2
  257.7 6.5 %collective-permute-done.50 = bf16[352,384]{1,0:T(8,128)(2,1)S(1)} collective-permute-done((bf16[352,384]{1,0:T(8,128)(2,1)S(1)}, bf16[352,384]{1,0:T(8,128)(2,1)S(1)}, u32[]{:S(2)}, u32[]{:S(2)}) %collective-permute-start.50) | collective-permute-done | bytes 270368 | tf_op jit(solution)/shard_map/ppermute | solution.py:351
  265.8 3.7 collective-permute-done.32
  272.5 2.2 collective-permute-start.52
  276.8 3.8 collective-permute-done.63
  280.7 2.9 collective-permute-start.34
  283.6 7.0 %collective-permute-done.62 = bf16[704,384]{1,0:T(8,128)(2,1)} collective-permute-done((bf16[704,384]{1,0:T(8,128)(2,1)}, bf16[704,384]{1,0:T(8,128)(2,1)}, u32[]{:S(2)}, u32[]{:S(2)}) %collective-permute-start.62) | collective-permute-done | bytes 540704 | tf_op jit(solution)/shard_map/ppermute | solution.py:351
  295.7 3.8 collective-permute-done.34
  302.8 7.9 %pull_blocks.4.rest_2_ = f32[64,192,128]{2,1,0:T(8,128)} custom-call(s32[2]{0:T(128)S(1)} %get-tuple-element.115.count_ref, s32[48]{0:T(128)S(1)} %reshape.517.block_ref, s32[48]{0:T(128)S(1)} %reshape.518.place_ref, s32[48]{0:T(128)S(1)} %tile.5.where_ref, bf16[2,24,80,128]{3,2,1,0:T(8,128)(2,1)S(1)} %copy-done.6, ...), custom_call_target="tpu_custom_call" | custom-call | tf_op jit(solution)/shard_map/pull_blocks/pallas_call | solution.py:306
  316.2 6.7 %collective-permute-done.56 = bf16[704,384]{1,0:T(8,128)(2,1)S(1)} collective-permute-done((bf16[704,384]{1,0:T(8,128)(2,1)S(1)}, bf16[704,384]{1,0:T(8,128)(2,1)S(1)}, u32[]{:S(2)}, u32[]{:S(2)}) %collective-permute-start.56) | collective-permute-done | bytes 540704 | tf_op jit(solution)/shard_map/ppermute | solution.py:351
  328.8 8.9 %collective-permute-done.60 = bf16[704,384]{1,0:T(8,128)(2,1)S(1)} collective-permute-done((bf16[704,384]{1,0:T(8,128)(2,1)S(1)}, bf16[704,384]{1,0:T(8,128)(2,1)S(1)}, u32[]{:S(2)}, u32[]{:S(2)}) %collective-permute-start.60) | collective-permute-done | bytes 540704 | tf_op jit(solution)/shard_map/ppermute | solution.py:351
  340.2 10.0 %pull_blocks.5.rest_2_ = f32[64,192,128]{2,1,0:T(8,128)} custom-call(s32[2]{0:T(128)S(1)} %get-tuple-element.116.count_ref, s32[48]{0:T(128)S(1)} %reshape.515.block_ref, s32[48]{0:T(128)S(1)} %reshape.516.place_ref, s32[48]{0:T(128)S(1)} %tile.5.where_ref, bf16[2,24,80,128]{3,2,1,0:T(8,128)(2,1)S(1)} %copy-done.4, ...), custom_call_target="tpu_custom_call" | custom-call | tf_op jit(solution)/shard_map/pull_blocks/pallas_call | solution.py:306
  351.6 5.6 %collective-permute-done.36 = bf16[704,384]{1,0:T(8,128)(2,1)} collective-permute-done((bf16[704,384]{1,0:T(8,128)(2,1)S(1)}, bf16[704,384]{1,0:T(8,128)(2,1)}, u32[]{:S(2)}, u32[]{:S(2)}) %collective-permute-start.36) | collective-permute-done | bytes 540704 | tf_op jit(solution)/shard_map/ppermute | solution.py:351
  362.3 10.3 %pull_blocks.6.rest_2_ = f32[64,192,128]{2,1,0:T(8,128)} custom-call(s32[2]{0:T(128)S(1)} %get-tuple-element.117.count_ref, s32[48]{0:T(128)S(1)} %reshape.513.block_ref, s32[48]{0:T(128)S(1)} %reshape.514.place_ref, s32[48]{0:T(128)S(1)} %tile.5.where_ref, bf16[2,24,80,128]{3,2,1,0:T(8,128)(2,1)S(1)} %copy-done.2, ...), custom_call_target="tpu_custom_call" | custom-call | tf_op jit(solution)/shard_map/pull_blocks/pallas_call | solution.py:306
  372.6 61.4 %all-reduce.4.cloned.1.call-done = f32[192,768]{1,0:T(8,128)} async-done(((f32[192,768]{1,0:T(8,128)}), f32[192,768]{1,0:T(8,128)}) %all-reduce.4.cloned.1.call-update) | async-done | bytes 589840 | tf_op jit(solution)/shard_map/psum | solution.py:453
  438.3 9.0 %pull_blocks.7 = bf16[64,192,128]{2,1,0:T(8,128)(2,1)} custom-call(s32[2]{0:T(128)S(1)} %get-tuple-element.118.count_ref, s32[48]{0:T(128)S(1)} %reshape.507.block_ref, s32[48]{0:T(128)S(1)} %reshape.508.place_ref, s32[48]{0:T(128)S(1)} %tile.5.where_ref, bf16[2,24,80,128]{3,2,1,0:T(8,128)(2,1)S(1)} %copy-done.8, ...), custom_call_target="tpu_custom_call" | custom-call | tf_op jit(solution)/shard_map/pull_blocks/pallas_call | solution.py:306
  (307 shorter events, 122.0 us)
Async XLA Ops:
  7.2 426.8 %all-reduce.4.cloned.1.call-start = ((), (), s32[]{:S(2)}) async-start(), calls=%async_computation | async-start | bytes 1179648 | tf_op jit(solution)/shard_map/psum | solution.py:453
  16.8 55.6 %collective-permute-start = (bf16[6,80,128]{2,1,0:T(8,128)(2,1)}, bf16[6,80,128]{2,1,0:T(8,128)(2,1)}, u32[]{:S(2)}, u32[]{:S(2)}) collective-permute-start(bf16[6,80,128]{2,1,0:T(8,128)(2,1)} %get-tuple-element.62), channel_id=1, source_target_pairs={{0,24},{4,28},{8,16},{12,20},{16,8},{20,12},{24,0},{28,4},{1,25},{... | collective-permute-start | bytes 368648 | tf_op jit(solution)/shard_map/ppermute | solution.py:351
  21.8 50.7 %collective-permute-start.1 = (bf16[6,80,128]{2,1,0:T(8,128)(2,1)}, bf16[6,80,128]{2,1,0:T(8,128)(2,1)}, u32[]{:S(2)}, u32[]{:S(2)}) collective-permute-start(bf16[6,80,128]{2,1,0:T(8,128)(2,1)} %get-tuple-element.61), channel_id=1, source_target_pairs={{0,28},{4,24},{8,20},{12,16},{16,12},{20,8},{24,4},{28,0},{1,29},{... | collective-permute-start | bytes 368648 | tf_op jit(solution)/shard_map/ppermute | solution.py:351
  23.0 52.9 %collective-permute-start.13 = (bf16[6,80,128]{2,1,0:T(8,128)(2,1)}, bf16[6,80,128]{2,1,0:T(8,128)(2,1)S(1)}, u32[]{:S(2)}, u32[]{:S(2)}) collective-permute-start(bf16[6,80,128]{2,1,0:T(8,128)(2,1)} %get-tuple-element.57), channel_id=1, source_target_pairs={{0,16},{4,20},{8,24},{12,28},{16,0},{20,4},{24,8},{28,12},{1,17},{... | collective-permute-start | bytes 368648 | tf_op jit(solution)/shard_map/ppermute | solution.py:351
  23.8 52.1 %collective-permute-start.14 = (bf16[6,80,128]{2,1,0:T(8,128)(2,1)}, bf16[6,80,128]{2,1,0:T(8,128)(2,1)}, u32[]{:S(2)}, u32[]{:S(2)}) collective-permute-start(bf16[6,80,128]{2,1,0:T(8,128)(2,1)} %get-tuple-element.56), channel_id=1, source_target_pairs={{0,20},{4,16},{8,28},{12,24},{16,4},{20,0},{24,12},{28,8},{1,21},{... | collective-permute-start | bytes 368648 | tf_op jit(solution)/shard_map/ppermute | solution.py:351
  25.7 51.7 %collective-permute-start.8 = (bf16[6,80,128]{2,1,0:T(8,128)(2,1)}, bf16[6,80,128]{2,1,0:T(8,128)(2,1)S(1)}, u32[]{:S(2)}, u32[]{:S(2)}) collective-permute-start(bf16[6,80,128]{2,1,0:T(8,128)(2,1)} %get-tuple-element.59), channel_id=1, source_target_pairs={{0,8},{4,12},{8,0},{12,4},{16,24},{20,28},{24,16},{28,20},{1,9},{5... | collective-permute-start | bytes 368648 | tf_op jit(solution)/shard_map/ppermute | solution.py:351
  77.5 16.5 %collective-permute-start.30 = (bf16[2,2,176,192]{3,2,1,0:T(8,128)(2,1)S(1)}, bf16[2,2,176,192]{3,2,1,0:T(8,128)(2,1)S(1)}, u32[]{:S(2)}, u32[]{:S(2)}) collective-permute-start(bf16[2,2,176,192]{3,2,1,0:T(8,128)(2,1)S(1)} %get-tuple-element.50), channel_id=1, source_target_pairs={{0,3},{1,2},{2,1},{3,0},{4,7},{5,6},{6,5},{7,4},{8,11},{9,10},{10,... | collective-permute-start | bytes 811016 | tf_op jit(solution)/shard_map/ppermute | solution.py:351
  79.4 20.9 %collective-permute-start.2 = (bf16[2,6,80,128]{3,2,1,0:T(8,128)(2,1)}, bf16[2,6,80,128]{3,2,1,0:T(8,128)(2,1)}, u32[]{:S(2)}, u32[]{:S(2)}) collective-permute-start(bf16[2,6,80,128]{3,2,1,0:T(8,128)(2,1)} %pad_maximum_fusion.20), channel_id=1, source_target_pairs={{0,2},{1,3},{2,0},{3,1},{4,6},{5,7},{6,4},{7,5},{8,10},{9,11},{10,... | collective-permute-start | bytes 737288 | tf_op jit(solution)/shard_map/ppermute | solution.py:351
  81.6 23.9 %collective-permute-start.15 = (bf16[2,6,80,128]{3,2,1,0:T(8,128)(2,1)}, bf16[2,6,80,128]{3,2,1,0:T(8,128)(2,1)}, u32[]{:S(2)}, u32[]{:S(2)}) collective-permute-start(bf16[2,6,80,128]{3,2,1,0:T(8,128)(2,1)} %pad_maximum_fusion.23), channel_id=1, source_target_pairs={{0,2},{1,3},{2,0},{3,1},{4,6},{5,7},{6,4},{7,5},{8,10},{9,11},{10,... | collective-permute-start | bytes 737288 | tf_op jit(solution)/shard_map/ppermute | solution.py:351
  82.9 27.9 %collective-permute-start.10 = (bf16[2,6,80,128]{3,2,1,0:T(8,128)(2,1)}, bf16[2,6,80,128]{3,2,1,0:T(8,128)(2,1)}, u32[]{:S(2)}, u32[]{:S(2)}) collective-permute-start(bf16[2,6,80,128]{3,2,1,0:T(8,128)(2,1)} %pad_maximum_fusion.22), channel_id=1, source_target_pairs={{0,2},{1,3},{2,0},{3,1},{4,6},{5,7},{6,4},{7,5},{8,10},{9,11},{10,... | collective-permute-start | bytes 737288 | tf_op jit(solution)/shard_map/ppermute | solution.py:351
  87.2 30.6 %collective-permute-start.5 = (bf16[2,6,80,128]{3,2,1,0:T(8,128)(2,1)}, bf16[2,6,80,128]{3,2,1,0:T(8,128)(2,1)}, u32[]{:S(2)}, u32[]{:S(2)}) collective-permute-start(bf16[2,6,80,128]{3,2,1,0:T(8,128)(2,1)} %pad_maximum_fusion.21), channel_id=1, source_target_pairs={{0,2},{1,3},{2,0},{3,1},{4,6},{5,7},{6,4},{7,5},{8,10},{9,11},{10,... | collective-permute-start | bytes 737288 | tf_op jit(solution)/shard_map/ppermute | solution.py:351
  111.8 18.4 %collective-permute-start.11 = (bf16[2,12,80,128]{3,2,1,0:T(8,128)(2,1)S(1)}, bf16[2,12,80,128]{3,2,1,0:T(8,128)(2,1)S(1)}, u32[]{:S(2)}, u32[]{:S(2)}) collective-permute-start(bf16[2,12,80,128]{3,2,1,0:T(8,128)(2,1)S(1)} %pad_maximum_fusion.18), channel_id=1, source_target_pairs={{0,1},{1,0},{2,3},{3,2},{4,5},{5,4},{6,7},{7,6},{8,9},{9,8},{10,11... | collective-permute-start | bytes 1474568 | tf_op jit(solution)/shard_map/ppermute | solution.py:351
  118.8 36.3 %collective-permute-start.6 = (bf16[2,12,80,128]{3,2,1,0:T(8,128)(2,1)S(1)}, bf16[2,12,80,128]{3,2,1,0:T(8,128)(2,1)}, u32[]{:S(2)}, u32[]{:S(2)}) collective-permute-start(bf16[2,12,80,128]{3,2,1,0:T(8,128)(2,1)S(1)} %pad_maximum_fusion.17), channel_id=1, source_target_pairs={{0,1},{1,0},{2,3},{3,2},{4,5},{5,4},{6,7},{7,6},{8,9},{9,8},{10,11... | collective-permute-start | bytes 1474568 | tf_op jit(solution)/shard_map/ppermute | solution.py:351
  119.3 25.1 %collective-permute-start.18 = (bf16[704,384]{1,0:T(8,128)(2,1)S(1)}, bf16[704,384]{1,0:T(8,128)(2,1)S(1)}, u32[]{:S(2)}, u32[]{:S(2)}) collective-permute-start(bf16[704,384]{1,0:T(8,128)(2,1)S(1)} %get-tuple-element.30), channel_id=1, source_target_pairs={{0,4},{4,0},{8,12},{12,8},{16,20},{20,16},{24,28},{28,24},{1,5},{5... | collective-permute-start | bytes 1622024 | tf_op jit(solution)/shard_map/ppermute | solution.py:351
  126.7 31.2 %collective-permute-start.40 = (bf16[704,384]{1,0:T(8,128)(2,1)S(1)}, bf16[704,384]{1,0:T(8,128)(2,1)S(1)}, u32[]{:S(2)}, u32[]{:S(2)}) collective-permute-start(bf16[704,384]{1,0:T(8,128)(2,1)S(1)} %get-tuple-element.37), channel_id=1, source_target_pairs={{0,4},{4,0},{8,12},{12,8},{16,20},{20,16},{24,28},{28,24},{1,5},{5... | collective-permute-start | bytes 1622024 | tf_op jit(solution)/shard_map/ppermute | solution.py:351
  130.2 37.4 %collective-permute-start.17 = (bf16[704,384]{1,0:T(8,128)(2,1)S(1)}, bf16[704,384]{1,0:T(8,128)(2,1)S(1)}, u32[]{:S(2)}, u32[]{:S(2)}) collective-permute-start(bf16[704,384]{1,0:T(8,128)(2,1)S(1)} %get-tuple-element.28), channel_id=1, source_target_pairs={{0,4},{4,0},{8,12},{12,8},{16,20},{20,16},{24,28},{28,24},{1,5},{5... | collective-permute-start | bytes 1622024 | tf_op jit(solution)/shard_map/ppermute | solution.py:351
  133.0 25.0 %collective-permute-start.42 = (bf16[704,384]{1,0:T(8,128)(2,1)S(1)}, bf16[704,384]{1,0:T(8,128)(2,1)S(1)}, u32[]{:S(2)}, u32[]{:S(2)}) collective-permute-start(bf16[704,384]{1,0:T(8,128)(2,1)S(1)} %fusion.1), channel_id=1, source_target_pairs={{0,8},{4,12},{24,16},{28,20},{1,9},{5,13},{25,17},{29,21},{2,10},{... | collective-permute-start | bytes 1622024 | tf_op jit(solution)/shard_map/ppermute | solution.py:351
  144.6 26.8 %collective-permute-start.19 = (bf16[704,384]{1,0:T(8,128)(2,1)S(1)}, bf16[704,384]{1,0:T(8,128)(2,1)S(1)}, u32[]{:S(2)}, u32[]{:S(2)}) collective-permute-start(bf16[704,384]{1,0:T(8,128)(2,1)S(1)} %fusion), channel_id=1, source_target_pairs={{0,8},{4,12},{24,16},{28,20},{1,9},{5,13},{25,17},{29,21},{2,10},{... | collective-permute-start | bytes 1622024 | tf_op jit(solution)/shard_map/ppermute | solution.py:351
  155.1 49.7 %collective-permute-start.26 = (bf16[192,768]{1,0:T(8,128)(2,1)S(1)}, bf16[192,768]{1,0:T(8,128)(2,1)S(1)}, u32[]{:S(2)}, u32[]{:S(2)}) collective-permute-start(bf16[192,768]{1,0:T(8,128)(2,1)S(1)} %copy-done.14), channel_id=1, source_target_pairs={{0,2},{1,3},{2,0},{3,1},{4,6},{5,7},{6,4},{7,5},{8,10},{9,11},{10,... | collective-permute-start | bytes 884744 | tf_op jit(solution)/shard_map/ppermute | solution.py:351
  157.9 37.6 %collective-permute-start.39 = (bf16[704,384]{1,0:T(8,128)(2,1)S(1)}, bf16[704,384]{1,0:T(8,128)(2,1)S(1)}, u32[]{:S(2)}, u32[]{:S(2)}) collective-permute-start(bf16[704,384]{1,0:T(8,128)(2,1)S(1)} %get-tuple-element.35), channel_id=1, source_target_pairs={{0,4},{4,0},{8,12},{12,8},{16,20},{20,16},{24,28},{28,24},{1,5},{5... | collective-permute-start | bytes 1622024 | tf_op jit(solution)/shard_map/ppermute | solution.py:351
  158.0 40.6 %collective-permute-start.12 = (bf16[704,384]{1,0:T(8,128)(2,1)S(1)}, bf16[704,384]{1,0:T(8,128)(2,1)S(1)}, u32[]{:S(2)}, u32[]{:S(2)}) collective-permute-start(bf16[704,384]{1,0:T(8,128)(2,1)S(1)} %get-tuple-element.26), channel_id=1, source_target_pairs={{0,4},{4,0},{8,12},{12,8},{16,20},{20,16},{24,28},{28,24},{1,5},{5... | collective-permute-start | bytes 1622024 | tf_op jit(solution)/shard_map/ppermute | solution.py:351
  167.6 16.4 %collective-permute-start.45 = (bf16[704,384]{1,0:T(8,128)(2,1)S(1)}, bf16[704,384]{1,0:T(8,128)(2,1)S(1)}, u32[]{:S(2)}, u32[]{:S(2)}) collective-permute-start(bf16[704,384]{1,0:T(8,128)(2,1)S(1)} %add_convert_fusion.3), channel_id=1, source_target_pairs={{0,8},{4,12},{24,16},{28,20},{1,9},{5,13},{25,17},{29,21},{2,10},{... | collective-permute-start | bytes 1622024 | tf_op jit(solution)/shard_map/ppermute | solution.py:351
  171.5 22.3 %collective-permute-start.22 = (bf16[704,384]{1,0:T(8,128)(2,1)S(1)}, bf16[704,384]{1,0:T(8,128)(2,1)S(1)}, u32[]{:S(2)}, u32[]{:S(2)}) collective-permute-start(bf16[704,384]{1,0:T(8,128)(2,1)S(1)} %add_convert_fusion.7), channel_id=1, source_target_pairs={{0,8},{4,12},{24,16},{28,20},{1,9},{5,13},{25,17},{29,21},{2,10},{... | collective-permute-start | bytes 1622024 | tf_op jit(solution)/shard_map/ppermute | solution.py:351
  195.5 18.4 %collective-permute-start.38 = (bf16[704,384]{1,0:T(8,128)(2,1)S(1)}, bf16[704,384]{1,0:T(8,128)(2,1)S(1)}, u32[]{:S(2)}, u32[]{:S(2)}) collective-permute-start(bf16[704,384]{1,0:T(8,128)(2,1)S(1)} %get-tuple-element.33), channel_id=1, source_target_pairs={{0,4},{4,0},{8,12},{12,8},{16,20},{20,16},{24,28},{28,24},{1,5},{5... | collective-permute-start | bytes 1622024 | tf_op jit(solution)/shard_map/ppermute | solution.py:351
  196.0 37.5 %collective-permute-start.7 = (bf16[704,384]{1,0:T(8,128)(2,1)}, bf16[704,384]{1,0:T(8,128)(2,1)}, u32[]{:S(2)}, u32[]{:S(2)}) collective-permute-start(bf16[704,384]{1,0:T(8,128)(2,1)} %get-tuple-element.24), channel_id=1, source_target_pairs={{0,4},{4,0},{8,12},{12,8},{16,20},{20,16},{24,28},{28,24},{1,5},{5... | collective-permute-start | bytes 1622024 | tf_op jit(solution)/shard_map/ppermute | solution.py:351
  198.6 31.7 %collective-permute-start.44 = (bf16[704,384]{1,0:T(8,128)(2,1)}, bf16[704,384]{1,0:T(8,128)(2,1)}, u32[]{:S(2)}, u32[]{:S(2)}) collective-permute-start(bf16[704,384]{1,0:T(8,128)(2,1)} %add_convert_fusion.2), channel_id=1, source_target_pairs={{0,8},{4,12},{8,0},{12,4},{16,24},{20,28},{24,16},{28,20},{1,9},{5... | collective-permute-start | bytes 1622024 | tf_op jit(solution)/shard_map/ppermute | solution.py:351
  202.3 28.1 %collective-permute-start.46 = (bf16[704,384]{1,0:T(8,128)(2,1)}, bf16[704,384]{1,0:T(8,128)(2,1)}, u32[]{:S(2)}, u32[]{:S(2)}) collective-permute-start(bf16[704,384]{1,0:T(8,128)(2,1)} %add_convert_fusion.1), channel_id=1, source_target_pairs={{8,16},{12,20},{16,8},{20,12},{9,17},{13,21},{17,9},{21,13},{10,18... | collective-permute-start | bytes 1622024 | tf_op jit(solution)/shard_map/ppermute | solution.py:351
  204.8 28.7 %collective-permute-start.21 = (bf16[704,384]{1,0:T(8,128)(2,1)}, bf16[704,384]{1,0:T(8,128)(2,1)}, u32[]{:S(2)}, u32[]{:S(2)}) collective-permute-start(bf16[704,384]{1,0:T(8,128)(2,1)} %add_convert_fusion.6), channel_id=1, source_target_pairs={{0,8},{4,12},{8,0},{12,4},{16,24},{20,28},{24,16},{28,20},{1,9},{5... | collective-permute-start | bytes 1622024 | tf_op jit(solution)/shard_map/ppermute | solution.py:351
  214.0 19.6 %collective-permute-start.23 = (bf16[704,384]{1,0:T(8,128)(2,1)}, bf16[704,384]{1,0:T(8,128)(2,1)}, u32[]{:S(2)}, u32[]{:S(2)}) collective-permute-start(bf16[704,384]{1,0:T(8,128)(2,1)} %add_convert_fusion.5), channel_id=1, source_target_pairs={{8,16},{12,20},{16,8},{20,12},{9,17},{13,21},{17,9},{21,13},{10,18... | collective-permute-start | bytes 1622024 | tf_op jit(solution)/shard_map/ppermute | solution.py:351
  265.2 15.5 %collective-permute-start.63 = (bf16[704,384]{1,0:T(8,128)(2,1)}, bf16[704,384]{1,0:T(8,128)(2,1)}, u32[]{:S(2)}, u32[]{:S(2)}) collective-permute-start(bf16[704,384]{1,0:T(8,128)(2,1)} %maximum_select_fusion.1), channel_id=1, source_target_pairs={{0,4},{4,0},{8,12},{12,8},{16,20},{20,16},{24,28},{28,24},{1,5},{5... | collective-permute-start | bytes 1622024 | tf_op jit(solution)/shard_map/ppermute | solution.py:351
  270.6 20.0 %collective-permute-start.62 = (bf16[704,384]{1,0:T(8,128)(2,1)}, bf16[704,384]{1,0:T(8,128)(2,1)}, u32[]{:S(2)}, u32[]{:S(2)}) collective-permute-start(bf16[704,384]{1,0:T(8,128)(2,1)} %maximum_select_fusion), channel_id=1, source_target_pairs={{0,4},{4,0},{8,12},{12,8},{16,20},{20,16},{24,28},{28,24},{1,5},{5... | collective-permute-start | bytes 1622024 | tf_op jit(solution)/shard_map/ppermute | solution.py:351
  272.4 38.3 %collective-permute-start.64 = (f32[2,192,768]{2,1,0:T(8,128)}, f32[2,192,768]{2,1,0:T(8,128)S(1)}, u32[]{:S(2)}, u32[]{:S(2)}) collective-permute-start(f32[2,192,768]{2,1,0:T(8,128)} %bitcast.79), channel_id=1, source_target_pairs={{0,1},{1,0},{2,3},{3,2},{4,5},{5,4},{6,7},{7,6},{8,9},{9,8},{10,11... | collective-permute-start | bytes 3538952 | tf_op jit(solution)/shard_map/ppermute | solution.py:351
  272.5 19.0 %collective-permute-start.52 = (bf16[704,384]{1,0:T(8,128)(2,1)}, bf16[704,384]{1,0:T(8,128)(2,1)}, u32[]{:S(2)}, u32[]{:S(2)}) collective-permute-start(bf16[704,384]{1,0:T(8,128)(2,1)} %maximum_select_fusion.1), channel_id=1, source_target_pairs={{0,8},{4,12},{8,0},{12,4},{16,24},{20,28},{24,16},{28,20},{1,9},{5... | collective-permute-start | bytes 1622024 | tf_op jit(solution)/shard_map/ppermute | solution.py:351
  274.7 18.3 %collective-permute-start.51 = (bf16[704,384]{1,0:T(8,128)(2,1)}, bf16[704,384]{1,0:T(8,128)(2,1)}, u32[]{:S(2)}, u32[]{:S(2)}) collective-permute-start(bf16[704,384]{1,0:T(8,128)(2,1)} %maximum_select_fusion.1), channel_id=1, source_target_pairs={{8,16},{12,20},{16,8},{20,12},{9,17},{13,21},{17,9},{21,13},{10,18... | collective-permute-start | bytes 1622024 | tf_op jit(solution)/shard_map/ppermute | solution.py:351
  280.7 18.8 %collective-permute-start.34 = (bf16[704,384]{1,0:T(8,128)(2,1)}, bf16[704,384]{1,0:T(8,128)(2,1)S(1)}, u32[]{:S(2)}, u32[]{:S(2)}) collective-permute-start(bf16[704,384]{1,0:T(8,128)(2,1)} %maximum_select_fusion), channel_id=1, source_target_pairs={{0,8},{4,12},{8,0},{12,4},{16,24},{20,28},{24,16},{28,20},{1,9},{5... | collective-permute-start | bytes 1622024 | tf_op jit(solution)/shard_map/ppermute | solution.py:351
  291.5 20.8 %collective-permute-start.53 = (bf16[704,384]{1,0:T(8,128)(2,1)}, bf16[704,384]{1,0:T(8,128)(2,1)}, u32[]{:S(2)}, u32[]{:S(2)}) collective-permute-start(bf16[704,384]{1,0:T(8,128)(2,1)} %collective-permute-done.52), channel_id=1, source_target_pairs={{8,16},{12,20},{16,8},{20,12},{9,17},{13,21},{17,9},{21,13},{10,18... | collective-permute-start | bytes 1622024 | tf_op jit(solution)/shard_map/ppermute | solution.py:351
  293.0 21.2 %collective-permute-start.58 = (bf16[704,384]{1,0:T(8,128)(2,1)}, bf16[704,384]{1,0:T(8,128)(2,1)S(1)}, u32[]{:S(2)}, u32[]{:S(2)}) collective-permute-start(bf16[704,384]{1,0:T(8,128)(2,1)} %collective-permute-done.51), channel_id=1, source_target_pairs={{8,0},{12,4},{16,24},{20,28},{9,1},{13,5},{17,25},{21,29},{10,2},{... | collective-permute-start | bytes 1622024 | tf_op jit(solution)/shard_map/ppermute | solution.py:351
  299.4 16.4 %collective-permute-start.35 = (bf16[704,384]{1,0:T(8,128)(2,1)S(1)}, bf16[704,384]{1,0:T(8,128)(2,1)S(1)}, u32[]{:S(2)}, u32[]{:S(2)}) collective-permute-start(bf16[704,384]{1,0:T(8,128)(2,1)S(1)} %collective-permute-done.34), channel_id=1, source_target_pairs={{8,16},{12,20},{16,8},{20,12},{9,17},{13,21},{17,9},{21,13},{10,18... | collective-permute-start | bytes 1622024 | tf_op jit(solution)/shard_map/ppermute | solution.py:351
  300.2 22.8 %collective-permute-start.56 = (bf16[704,384]{1,0:T(8,128)(2,1)S(1)}, bf16[704,384]{1,0:T(8,128)(2,1)S(1)}, u32[]{:S(2)}, u32[]{:S(2)}) collective-permute-start(bf16[704,384]{1,0:T(8,128)(2,1)S(1)} %collective-permute-done.33), channel_id=1, source_target_pairs={{8,0},{12,4},{16,24},{20,28},{9,1},{13,5},{17,25},{21,29},{10,2},{... | collective-permute-start | bytes 1622024 | tf_op jit(solution)/shard_map/ppermute | solution.py:351
  310.7 15.4 %collective-permute-start.61 = (bf16[704,384]{1,0:T(8,128)(2,1)}, bf16[704,384]{1,0:T(8,128)(2,1)S(1)}, u32[]{:S(2)}, u32[]{:S(2)}) collective-permute-start(bf16[704,384]{1,0:T(8,128)(2,1)} %collective-permute-done.52), channel_id=1, source_target_pairs={{0,4},{4,0},{8,12},{12,8},{16,20},{20,16},{24,28},{28,24},{1,5},{5... | collective-permute-start | bytes 1622024 | tf_op jit(solution)/shard_map/ppermute | solution.py:351
  312.3 25.3 %collective-permute-start.60 = (bf16[704,384]{1,0:T(8,128)(2,1)S(1)}, bf16[704,384]{1,0:T(8,128)(2,1)S(1)}, u32[]{:S(2)}, u32[]{:S(2)}) collective-permute-start(bf16[704,384]{1,0:T(8,128)(2,1)S(1)} %collective-permute-done.34), channel_id=1, source_target_pairs={{0,4},{4,0},{8,12},{12,8},{16,20},{20,16},{24,28},{28,24},{1,5},{5... | collective-permute-start | bytes 1622024 | tf_op jit(solution)/shard_map/ppermute | solution.py:351
  314.2 35.9 %collective-permute-start.65 = (f32[192,768]{1,0:T(8,128)S(1)}, f32[192,768]{1,0:T(8,128)S(1)}, u32[]{:S(2)}, u32[]{:S(2)}) collective-permute-start(f32[192,768]{1,0:T(8,128)S(1)} %slice_bitcast_fusion), channel_id=1, source_target_pairs={{0,2},{1,3},{2,0},{3,1},{4,6},{5,7},{6,4},{7,5},{8,10},{9,11},{10,... | collective-permute-start | bytes 1769480 | tf_op jit(solution)/shard_map/ppermute | solution.py:351
  315.8 42.6 %collective-permute-start.59 = (bf16[704,384]{1,0:T(8,128)(2,1)S(1)}, bf16[704,384]{1,0:T(8,128)(2,1)}, u32[]{:S(2)}, u32[]{:S(2)}) collective-permute-start(bf16[704,384]{1,0:T(8,128)(2,1)S(1)} %broadcast_select_fusion.1), channel_id=1, source_target_pairs={{0,4},{4,0},{8,12},{12,8},{16,20},{20,16},{24,28},{28,24},{1,5},{5... | collective-permute-start | bytes 1622024 | tf_op jit(solution)/shard_map/ppermute | solution.py:351
  323.0 38.0 %collective-permute-start.57 = (bf16[704,384]{1,0:T(8,128)(2,1)S(1)}, bf16[704,384]{1,0:T(8,128)(2,1)}, u32[]{:S(2)}, u32[]{:S(2)}) collective-permute-start(bf16[704,384]{1,0:T(8,128)(2,1)S(1)} %broadcast_select_fusion.2), channel_id=1, source_target_pairs={{0,4},{4,0},{8,12},{12,8},{16,20},{20,16},{24,28},{28,24},{1,5},{5... | collective-permute-start | bytes 1622024 | tf_op jit(solution)/shard_map/ppermute | solution.py:351
  326.1 25.0 %collective-permute-start.54 = (bf16[704,384]{1,0:T(8,128)(2,1)}, bf16[704,384]{1,0:T(8,128)(2,1)S(1)}, u32[]{:S(2)}, u32[]{:S(2)}) collective-permute-start(bf16[704,384]{1,0:T(8,128)(2,1)} %collective-permute-done.53), channel_id=1, source_target_pairs={{8,0},{12,4},{16,24},{20,28},{9,1},{13,5},{17,25},{21,29},{10,2},{... | collective-permute-start | bytes 1622024 | tf_op jit(solution)/shard_map/ppermute | solution.py:351
  337.7 19.6 %collective-permute-start.36 = (bf16[704,384]{1,0:T(8,128)(2,1)S(1)}, bf16[704,384]{1,0:T(8,128)(2,1)}, u32[]{:S(2)}, u32[]{:S(2)}) collective-permute-start(bf16[704,384]{1,0:T(8,128)(2,1)S(1)} %collective-permute-done.35), channel_id=1, source_target_pairs={{8,0},{12,4},{16,24},{20,28},{9,1},{13,5},{17,25},{21,29},{10,2},{... | collective-permute-start | bytes 1622024 | tf_op jit(solution)/shard_map/ppermute | solution.py:351
  351.2 84.7 %collective-permute-start.55 = (bf16[704,384]{1,0:T(8,128)(2,1)S(1)}, bf16[704,384]{1,0:T(8,128)(2,1)}, u32[]{:S(2)}, u32[]{:S(2)}) collective-permute-start(bf16[704,384]{1,0:T(8,128)(2,1)S(1)} %broadcast_select_fusion.3), channel_id=1, source_target_pairs={{0,4},{4,0},{8,12},{12,8},{16,20},{20,16},{24,28},{28,24},{1,5},{5... | collective-permute-start | bytes 1622024 | tf_op jit(solution)/shard_map/ppermute | solution.py:351
  358.4 78.7 %collective-permute-start.37 = (bf16[704,384]{1,0:T(8,128)(2,1)S(1)}, bf16[704,384]{1,0:T(8,128)(2,1)S(1)}, u32[]{:S(2)}, u32[]{:S(2)}) collective-permute-start(bf16[704,384]{1,0:T(8,128)(2,1)S(1)} %broadcast_select_fusion.4), channel_id=1, source_target_pairs={{0,4},{4,0},{8,12},{12,8},{16,20},{20,16},{24,28},{28,24},{1,5},{5... | collective-permute-start | bytes 1622024 | tf_op jit(solution)/shard_map/ppermute | solution.py:351
  (53 other events, 436.4 us)
Sparse Core Ops, SparseCore 0:
  351.2 82.7 all-reduce.3
